TPU v7x, 32 devices: a whole 2x2x4 slice. The times are simulated.
32 devices in a mesh: groups: 2 (over y), tok: 4 (over z), col: 4 (over x, core).
Axes of the slice: x: 2, y: 2, z: 4, core: 2. Of those that a mesh axis runs over, the one named last changes fastest.
Arguments:
- attn_out: bfloat16 [512, 8192], P(('groups', 'tok'), 'col'), parts along dimension 0, may hold values from -12 to 12
- residual: bfloat16 [512, 8192], P(('groups', 'col'), 'tok'), parts along dimension 0, may hold values from -310 to 310
- w_out: bfloat16 [8192, 8192], P('col', 'tok'), may hold values from -0.0625 to 0.0625
- norm_gain: float32 [8192], P('tok'), may hold values from 0.5 to 1.5
- rotation: bfloat16 [8192, 8192], P('tok', 'col'), may hold values from -0.23201941 to 0.23201941
Outputs:
- kurtosis: float32 [512], P(('groups', 'tok')), parts along dimension 0
- grad_rot: float32 [16384, 8192], P(('groups', 'tok'), 'col'), parts along dimension 0
There are 2 independent parts, one for each index of `groups`. A program takes and returns all parts, laid end to end along the dimension named above; an argument that names none is the same for every part. Nothing has to cross between parts.
All inputs are finite; a program needn't handle non-finite values.
Results may differ from a plain program's by a relative error of at most 0.0018.
The roundings to bfloat16 on the way count: a program that leaves them out, or rounds other values in their place, can miss the bound.
Values may be sent and summed in bfloat16 or wider, within the bound.
A program may use at most 128 MiB of HBM per device.

v0:
```python
import math
import jax
import jax.numpy as jnp
from jax import lax
from jax.sharding import PartitionSpec as P

norm_eps = 1e-05
moment_eps = 1e-06


def kurtosis_terms(rotated, second, fourth, full_width):
    moment_two = second / full_width + moment_eps
    kurt_vals = fourth / full_width / (moment_two * moment_two)
    cubed = rotated * rotated * rotated
    grad_vals = (
        cubed / (moment_two * moment_two)[:, None] - (kurt_vals / moment_two)[:, None] * rotated
    )
    return (kurt_vals, grad_vals.astype(jnp.bfloat16))


def power_sums(rotated, along):
    squares = rotated * rotated
    return (jnp.sum(squares, axis=along), jnp.sum(squares * squares, axis=along))


def shards(attn_out, residual, w_out, norm_gain, rotation):
    heads_all = lax.all_gather(attn_out, "tok", axis=0, tiled=True)
    row_block = heads_all
    projected = lax.psum_scatter(
        jnp.dot(row_block, w_out, preferred_element_type=jnp.float32),
        "col",
        scatter_dimension=0,
        tiled=True,
    )
    hidden = residual.astype(jnp.float32) + projected
    square_sum = lax.psum(jnp.sum(hidden * hidden, axis=1), "tok")
    full_width = hidden.shape[1] * lax.axis_size("tok")
    row_scale = lax.rsqrt(square_sum / full_width + norm_eps)
    normed = (hidden * row_scale[:, None] * norm_gain[None, :]).astype(jnp.bfloat16)
    normed_all = lax.all_gather(normed, "col", axis=0, tiled=True)
    tokens_total = normed_all.shape[0]
    row_block = normed_all
    rotated = lax.psum_scatter(
        jnp.dot(row_block, rotation, preferred_element_type=jnp.float32),
        "tok",
        scatter_dimension=0,
        tiled=True,
    )
    second, fourth = lax.psum(power_sums(rotated, 1), "col")
    kurt_vals, grad_own = kurtosis_terms(rotated, second, fourth, full_width)
    grad_all = lax.all_gather(grad_own, "tok", axis=0, tiled=True)
    grad_rot = lax.dot_general(
        normed_all, grad_all, (((0,), (0,)), ((), ())), preferred_element_type=jnp.float32
    )
    return (kurt_vals, grad_rot / math.sqrt(tokens_total))


def solution(mesh):
    return jax.shard_map(
        shards,
        mesh=mesh,
        in_specs=(
            P(("groups", "tok"), "col"),
            P(("groups", "col"), "tok"),
            P("col", "tok"),
            P("tok"),
            P("tok", "col"),
        ),
        out_specs=(P(("groups", "tok")), P(("groups", "tok"), "col")),
        check_vma=False,
    )
```

profile of v0, /device:TPU:0, one launch (start us, length us, event | category | flops | bytes accessed | tf_op | source)
XLA Modules:
  0.0 212.4 jit_solution(18247029739795986867)
XLA Ops:
  7.2 0.0 all-gather.4.cloned.1.call-start
  7.2 0.7 all-gather.4.cloned.1.call-update
  7.9 0.0 reduce-scatter.3.cloned.1.call-start
  8.0 32.3 %all-gather.4.cloned.1.call-done = bf16[256,2048]{1,0:T(8,128)(2,1)} async-done(((bf16[64,2048]{1,0:T(8,128)(2,1)}), bf16[256,2048]{1,0:T(8,128)(2,1)}) %all-gather.4.cloned.1.call-update) | async-done | bytes 1048592 | tf_op jit(solution)/shard_map/all_gather | solution.py:27
  40.2 7.4 %fusion.5 = f32[256,2048]{1,0:T(8,128)} fusion(bf16[256,2048]{1,0:T(8,128)(2,1)} %all-gather.4.cloned.1.call-done, bf16[2048,2048]{1,0:T(8,128)(2,1)} %param.7), kind=kOutput, calls=%fused_computation.16 | convolution fusion | flops 2147483648 | bytes 11534336 | tf_op jit(solution)/shard_map/dot_general | solution.py:30
  47.6 0.0 reduce-scatter.3.cloned.1.call-update
  47.6 0.0 all-gather.6.cloned.1.call-start
  47.7 31.0 %reduce-scatter.3.cloned.1.call-done = f32[64,2048]{1,0:T(8,128)} async-done(((f32[256,2048]{1,0:T(8,128)}), f32[64,2048]{1,0:T(8,128)}) %reduce-scatter.3.cloned.1.call-update) | async-done | bytes 524304 | tf_op jit(solution)/shard_map/reduce_scatter | solution.py:29
  78.7 1.2 multiply_reduce_fusion.1
  79.9 11.7 %psum.21 = f32[64]{0:T(128)S(1)} all-reduce(f32[64]{0:T(128)S(1)} %multiply_reduce_fusion.1), channel_id=1, replica_groups=mesh['groups'=2,'tok'=4,'col'=4] {'tok'}, use_global_device_ids=true, to_apply=%region_2.0 | all-reduce | flops 64 | bytes 512 | tf_op jit(solution)/shard_map/psum | solution.py:36
  91.6 1.9 multiply_convert_fusion
  93.5 0.0 all-gather.6.cloned.1.call-update
  93.5 0.0 reduce-scatter.5.cloned.1.call-start
  93.6 14.1 %all-gather.6.cloned.1.call-done = bf16[256,2048]{1,0:T(8,128)(2,1)} async-done(((bf16[64,2048]{1,0:T(8,128)(2,1)}), bf16[256,2048]{1,0:T(8,128)(2,1)}) %all-gather.6.cloned.1.call-update) | async-done | bytes 1048592 | tf_op jit(solution)/shard_map/all_gather | solution.py:40
  107.6 7.4 %fusion.6 = f32[256,2048]{1,0:T(8,128)} fusion(bf16[256,2048]{1,0:T(8,128)(2,1)} %all-gather.6.cloned.1.call-done, bf16[2048,2048]{1,0:T(8,128)(2,1)} %param.9), kind=kOutput, calls=%fused_computation.17 | convolution fusion | flops 2147483648 | bytes 11534336 | tf_op jit(solution)/shard_map/dot_general | solution.py:44
  115.1 0.0 reduce-scatter.5.cloned.1.call-update
  115.1 0.0 all-gather.8.cloned.1.call-start
  115.1 44.0 %reduce-scatter.5.cloned.1.call-done = f32[64,2048]{1,0:T(8,128)} async-done(((f32[256,2048]{1,0:T(8,128)}), f32[64,2048]{1,0:T(8,128)}) %reduce-scatter.5.cloned.1.call-update) | async-done | bytes 524304 | tf_op jit(solution)/shard_map/reduce_scatter | solution.py:43
  159.1 1.2 multiply_reduce_fusion
  160.3 6.4 %all-reduce = (f32[64]{0:T(128)S(1)}, f32[64]{0:T(128)S(1)}) all-reduce(f32[64]{0:T(128)S(1)} %get-tuple-element.3, f32[64]{0:T(128)S(1)} %get-tuple-element.2), channel_id=1, replica_groups=mesh['groups'=2,'tok'=4,'col'=4] {'col'}, use_global_device_ids=true, to_apply=%region_5.0 | all-reduce | flops 128 | bytes 1024 | tf_op jit(solution)/shard_map/psum | solution.py:49
  166.7 0.5 multiply_divide_fusion
  167.2 1.9 fusion.3
  169.2 27.0 %all-gather.8.cloned.1.call-done = bf16[256,2048]{1,0:T(8,128)(2,1)} async-done(((bf16[64,2048]{1,0:T(8,128)(2,1)}), bf16[256,2048]{1,0:T(8,128)(2,1)}) %all-gather.8.cloned.1.call-update) | async-done | bytes 1048592 | tf_op jit(solution)/shard_map/all_gather | solution.py:51
  196.1 9.8 %convolution_multiply_fusion = f32[2048,2048]{1,0:T(8,128)} fusion(bf16[256,2048]{1,0:T(8,128)(2,1)S(1)} %copy-done, bf16[256,2048]{1,0:T(8,128)(2,1)} %all-gather.8.cloned.1.call-done), kind=kOutput, calls=%fused_computation | convolution fusion | flops 2151677952 | bytes 18874368 | tf_op jit(solution)/shard_map/dot_general | solution.py:52
  (8 shorter events, 0.0 us)
Async XLA Ops:
  7.2 33.1 %all-gather.4.cloned.1.call-start = ((), (), s32[]{:S(2)}) async-start(), calls=%async_computation.2 | async-start | bytes 1310720 | tf_op jit(solution)/shard_map/all_gather | solution.py:27
  7.9 70.8 %copy-start.1 = (bf16[64,2048]{1,0:T(8,128)(2,1)S(1)}, bf16[64,2048]{1,0:T(8,128)(2,1)}, u32[]{:S(2)}) copy-start(bf16[64,2048]{1,0:T(8,128)(2,1)} %param.6) | copy-start | bytes 786436
  7.9 83.7 %copy-start.2 = (f32[2048]{0:T(1024)S(1)}, f32[2048]{0:T(1024)}, u32[]{:S(2)}) copy-start(f32[2048]{0:T(1024)} %param.8) | copy-start | bytes 24580
  7.9 70.8 %reduce-scatter.3.cloned.1.call-start = ((), (), s32[]{:S(2)}) async-start(), calls=%async_computation.3 | async-start | bytes 2621440 | tf_op jit(solution)/shard_map/reduce_scatter | solution.py:29
  47.6 60.0 %all-gather.6.cloned.1.call-start = ((), (), s32[]{:S(2)}) async-start(), calls=%async_computation.4 | async-start | bytes 1310720 | tf_op jit(solution)/shard_map/all_gather | solution.py:40
  93.5 65.6 %reduce-scatter.5.cloned.1.call-start = ((), (), s32[]{:S(2)}) async-start(), calls=%async_computation.5 | async-start | bytes 2621440 | tf_op jit(solution)/shard_map/reduce_scatter | solution.py:43
  107.6 88.5 %copy-start = (bf16[256,2048]{1,0:T(8,128)(2,1)S(1)}, bf16[256,2048]{1,0:T(8,128)(2,1)}, u32[]{:S(2)}) copy-start(bf16[256,2048]{1,0:T(8,128)(2,1)} %all-gather.6.cloned.1.call-done) | copy-start | bytes 3145732
  115.1 81.0 %all-gather.8.cloned.1.call-start = ((), (), s32[]{:S(2)}) async-start(), calls=%async_computation.6 | async-start | bytes 1310720 | tf_op jit(solution)/shard_map/all_gather | solution.py:51
Sparse Core Ops, SparseCore 0:
  9.6 30.6 all-gather.3
  47.7 30.9 reduce-scatter.2
  93.6 13.9 all-gather.5
  115.2 43.8 reduce-scatter.4
  169.3 26.7 all-gather.7
where the time goes:
time: 213 us; the launch traced here: 212 us
  waiting for transfers between devices  149 us (70%)
  matrix products  24.6 us (12%)
  blocking collectives  18.1 us (8%)
  between operations  13.8 us (6%)
  other arithmetic  6.69 us (3%)
    reduce_scatter x1, waiting for transfers between devices, shards(): lax.psum_scatter(jnp.dot(row_block, rotation, preferred_element_type=jnp....  44 us
    all_gather x1, waiting for transfers between devices, shards(): heads_all = lax.all_gather(attn_out, 'tok', axis=0, tiled=True)  32.3 us
    reduce_scatter x1, waiting for transfers between devices, shards(): lax.psum_scatter(jnp.dot(row_block, w_out, preferred_element_type=jnp.flo...  31 us
    all_gather x1, waiting for transfers between devices, shards(): grad_all = lax.all_gather(grad_own, 'tok', axis=0, tiled=True)  27 us
    all_gather x1, waiting for transfers between devices, shards(): normed_all = lax.all_gather(normed, 'col', axis=0, tiled=True)  14.1 us
    psum x1, blocking collectives, shards(): square_sum = lax.psum(jnp.sum(hidden * hidden, axis=1), 'tok')  11.7 us
    dot_general x1, matrix products, shards(): lax.dot_general(normed_all, grad_all, (((0,), (0,)), ((), ())), preferred...  9.77 us
    dot_general x1, matrix products, shards(): jnp.dot(row_block, rotation, preferred_element_type=jnp.float32)  7.44 us
  transfers between devices with their start and end apart: 5, of which 5 were waited for; matrix products, arithmetic and copies ran while one was open for 0% of the time, Pallas kernels for 0%

commit v1 on v0

--- a/solution.py
+++ b/solution.py
@@ -6,6 +6,24 @@
 
 norm_eps = 1e-05
 moment_eps = 1e-06
+
+
+def joined_along(pieces, dim):
+    pieces = jnp.moveaxis(pieces, 0, dim)
+    lengths = pieces.shape
+    return pieces.reshape(*lengths[:dim], lengths[dim] * lengths[dim + 1], *lengths[dim + 2 :])
+
+
+def grow_blocks(x, axis):
+    length = lax.axis_size(axis)
+    parts = x[None]
+    for level in range(length.bit_length() - 1):
+        distance = 1 << level
+        partner_block = lax.ppermute(parts, axis, [(i, i ^ distance) for i in range(length)])
+        both = jnp.stack([parts, partner_block])
+        upper = lax.axis_index(axis) >> level & 1
+        parts = jnp.where(upper == 0, both, both[::-1]).reshape(-1, *x.shape)
+    return parts
 
 
 def kurtosis_terms(rotated, second, fourth, full_width):
@@ -24,7 +42,7 @@
 
 
 def shards(attn_out, residual, w_out, norm_gain, rotation):
-    heads_all = lax.all_gather(attn_out, "tok", axis=0, tiled=True)
+    heads_all = joined_along(grow_blocks(attn_out, "tok"), 0)
     row_block = heads_all
     projected = lax.psum_scatter(
         jnp.dot(row_block, w_out, preferred_element_type=jnp.float32),

time: 213 us -> 217 us (1.019)
  starting transfers between devices: 0.2 us -> 6.07 us
    all_gather x1 -> x0, waiting for transfers between devices: 32.3 us -> none  [shards(): heads_all = lax.all_gather(attn_out, 'tok', axis=0, tiled=True)]
    ppermute x0 -> x2, waiting for transfers between devices: none -> 29 us  [grow_blocks(): lax.ppermute(parts, axis, [(i, i ^ distance) for i in range(length)])]
    ppermute x0 -> x2, starting transfers between devices: none -> 5.91 us  [grow_blocks(): lax.ppermute(parts, axis, [(i, i ^ distance) for i in range(length)])]
  transfers between devices with their start and end apart: 5 -> 6, of which waited for: 5 -> 6; matrix products, arithmetic and copies ran while one was open for 0% -> 0% of each run, Pallas kernels for 0% -> 0%
where the time goes in v1:
time: 217 us
  waiting for transfers between devices  147 us (68%)
  matrix products  24.3 us (11%)
  blocking collectives  18.1 us (8%)
  between operations  13.8 us (6%)
  other arithmetic  8.2 us (4%)
  starting transfers between devices  6.07 us (3%)
    reduce_scatter x1, waiting for transfers between devices, shards(): lax.psum_scatter(jnp.dot(row_block, rotation, preferred_element_type=jnp....  44 us
    reduce_scatter x1, waiting for transfers between devices, shards(): lax.psum_scatter(jnp.dot(row_block, w_out, preferred_element_type=jnp.flo...  32.5 us
    ppermute x2, waiting for transfers between devices, grow_blocks(): lax.ppermute(parts, axis, [(i, i ^ distance) for i in range(length)])  29 us
    all_gather x1, waiting for transfers between devices, shards(): grad_all = lax.all_gather(grad_own, 'tok', axis=0, tiled=True)  27 us
    all_gather x1, waiting for transfers between devices, shards(): normed_all = lax.all_gather(normed, 'col', axis=0, tiled=True)  14.1 us
    psum x1, blocking collectives, shards(): square_sum = lax.psum(jnp.sum(hidden * hidden, axis=1), 'tok')  11.7 us
    dot_general x1, matrix products, shards(): lax.dot_general(normed_all, grad_all, (((0,), (0,)), ((), ())), preferred...  9.77 us
    dot_general x1, matrix products, shards(): jnp.dot(row_block, rotation, preferred_element_type=jnp.float32)  7.44 us
  transfers between devices with their start and end apart: 6, of which 6 were waited for; matrix products, arithmetic and copies ran while one was open for 0% of the time, Pallas kernels for 0%

profile of v1, /device:TPU:0, one launch (start us, length us, event | category | flops | bytes accessed | tf_op | source)
XLA Modules:
  0.0 217.1 jit_solution(6291237802757774495)
XLA Ops:
  7.2 3.1 %collective-permute-start = (bf16[1,64,2048]{2,1,0:T(8,128)(2,1)}, bf16[1,64,2048]{2,1,0:T(8,128)(2,1)S(1)}, u32[]{:S(2)}, u32[]{:S(2)}) collective-permute-start(bf16[1,64,2048]{2,1,0:T(8,128)(2,1)} %bitcast.17), channel_id=1, source_target_pairs={{0,4},{4,0},{8,12},{12,8},{1,5},{5,1},{9,13},{13,9},{2,6},{6,2},{1... | collective-permute-start | bytes 786440 | tf_op jit(solution)/shard_map/ppermute | solution.py:22
  10.3 6.5 %collective-permute-done = bf16[1,64,2048]{2,1,0:T(8,128)(2,1)S(1)} collective-permute-done((bf16[1,64,2048]{2,1,0:T(8,128)(2,1)}, bf16[1,64,2048]{2,1,0:T(8,128)(2,1)S(1)}, u32[]{:S(2)}, u32[]{:S(2)}) %collective-permute-start) | collective-permute-done | bytes 262176 | tf_op jit(solution)/shard_map/ppermute | solution.py:22
  16.8 1.0 pad_maximum_fusion.1
  17.8 0.1 fusion.5
  18.0 2.8 %collective-permute-start.1 = (bf16[2,64,2048]{2,1,0:T(8,128)(2,1)S(1)}, bf16[2,64,2048]{2,1,0:T(8,128)(2,1)S(1)}, u32[]{:S(2)}, u32[]{:S(2)}) collective-permute-start(bf16[2,64,2048]{2,1,0:T(8,128)(2,1)S(1)} %get-tuple-element.7), channel_id=1, source_target_pairs={{0,8},{4,12},{8,0},{12,4},{1,9},{5,13},{9,1},{13,5},{2,10},{6,14},... | collective-permute-start | bytes 1572872 | tf_op jit(solution)/shard_map/ppermute | solution.py:22
  20.8 22.5 %collective-permute-done.1 = bf16[2,64,2048]{2,1,0:T(8,128)(2,1)S(1)} collective-permute-done((bf16[2,64,2048]{2,1,0:T(8,128)(2,1)S(1)}, bf16[2,64,2048]{2,1,0:T(8,128)(2,1)S(1)}, u32[]{:S(2)}, u32[]{:S(2)}) %collective-permute-start.1) | collective-permute-done | bytes 524320 | tf_op jit(solution)/shard_map/ppermute | solution.py:22
  43.3 0.1 pad_maximum_fusion
  43.4 0.3 reverse_select_fusion
  43.7 7.1 %fusion.7 = f32[256,2048]{1,0:T(8,128)} fusion(bf16[256,2048]{1,0:T(8,128)(2,1)S(1)} %bitcast.15, bf16[2048,2048]{1,0:T(8,128)(2,1)} %param.7), kind=kOutput, calls=%fused_computation.22 | convolution fusion | flops 2147483648 | bytes 11534336 | tf_op jit(solution)/shard_map/dot_general | solution.py:48
  50.8 0.0 all-gather.3.cloned.1.call-start
  50.9 32.5 %reduce-scatter.3.cloned.1.call-done = f32[64,2048]{1,0:T(8,128)} async-done(((f32[256,2048]{1,0:T(8,128)}), f32[64,2048]{1,0:T(8,128)}) %reduce-scatter.3.cloned.1.call-update) | async-done | bytes 524304 | tf_op jit(solution)/shard_map/reduce_scatter | solution.py:47
  83.4 1.2 multiply_reduce_fusion.1
  84.6 11.7 %psum.21 = f32[64]{0:T(128)S(1)} all-reduce(f32[64]{0:T(128)S(1)} %multiply_reduce_fusion.1), channel_id=1, replica_groups=mesh['groups'=2,'tok'=4,'col'=4] {'tok'}, use_global_device_ids=true, to_apply=%region_2.3 | all-reduce | flops 64 | bytes 512 | tf_op jit(solution)/shard_map/psum | solution.py:54
  96.3 1.9 multiply_convert_fusion
  98.2 14.1 %all-gather.3.cloned.1.call-done = bf16[256,2048]{1,0:T(8,128)(2,1)} async-done(((bf16[64,2048]{1,0:T(8,128)(2,1)}), bf16[256,2048]{1,0:T(8,128)(2,1)}) %all-gather.3.cloned.1.call-update) | async-done | bytes 1048592 | tf_op jit(solution)/shard_map/all_gather | solution.py:58
  112.3 7.4 %fusion.8 = f32[256,2048]{1,0:T(8,128)} fusion(bf16[256,2048]{1,0:T(8,128)(2,1)} %all-gather.3.cloned.1.call-done, bf16[2048,2048]{1,0:T(8,128)(2,1)} %param.9), kind=kOutput, calls=%fused_computation.23 | convolution fusion | flops 2147483648 | bytes 11534336 | tf_op jit(solution)/shard_map/dot_general | solution.py:62
  119.7 0.0 all-gather.5.cloned.1.call-start
  119.8 44.0 %reduce-scatter.5.cloned.1.call-done = f32[64,2048]{1,0:T(8,128)} async-done(((f32[256,2048]{1,0:T(8,128)}), f32[64,2048]{1,0:T(8,128)}) %reduce-scatter.5.cloned.1.call-update) | async-done | bytes 524304 | tf_op jit(solution)/shard_map/reduce_scatter | solution.py:61
  163.8 1.2 multiply_reduce_fusion
  165.0 6.4 %all-reduce = (f32[64]{0:T(128)S(1)}, f32[64]{0:T(128)S(1)}) all-reduce(f32[64]{0:T(128)S(1)} %get-tuple-element.3, f32[64]{0:T(128)S(1)} %get-tuple-element.2), channel_id=1, replica_groups=mesh['groups'=2,'tok'=4,'col'=4] {'col'}, use_global_device_ids=true, to_apply=%region_5.6 | all-reduce | flops 128 | bytes 1024 | tf_op jit(solution)/shard_map/psum | solution.py:67
  171.4 0.5 multiply_divide_fusion
  171.9 1.9 fusion.3
  173.8 27.0 %all-gather.5.cloned.1.call-done = bf16[256,2048]{1,0:T(8,128)(2,1)} async-done(((bf16[64,2048]{1,0:T(8,128)(2,1)}), bf16[256,2048]{1,0:T(8,128)(2,1)}) %all-gather.5.cloned.1.call-update) | async-done | bytes 1048592 | tf_op jit(solution)/shard_map/all_gather | solution.py:69
  200.8 9.8 %convolution_multiply_fusion = f32[2048,2048]{1,0:T(8,128)} fusion(bf16[256,2048]{1,0:T(8,128)(2,1)S(1)} %copy-done, bf16[256,2048]{1,0:T(8,128)(2,1)} %all-gather.5.cloned.1.call-done), kind=kOutput, calls=%fused_computation | convolution fusion | flops 2151677952 | bytes 18874368 | tf_op jit(solution)/shard_map/dot_general | solution.py:70
  (13 shorter events, 0.2 us)
Async XLA Ops:
  7.2 76.2 %reduce-scatter.3.cloned.1.call-start = ((), (), s32[]{:S(2)}) async-start(), calls=%async_computation.2 | async-start | bytes 2621440 | tf_op jit(solution)/shard_map/reduce_scatter | solution.py:47
  7.2 9.6 %collective-permute-start = (bf16[1,64,2048]{2,1,0:T(8,128)(2,1)}, bf16[1,64,2048]{2,1,0:T(8,128)(2,1)S(1)}, u32[]{:S(2)}, u32[]{:S(2)}) collective-permute-start(bf16[1,64,2048]{2,1,0:T(8,128)(2,1)} %bitcast.17), channel_id=1, source_target_pairs={{0,4},{4,0},{8,12},{12,8},{1,5},{5,1},{9,13},{13,9},{2,6},{6,2},{1... | collective-permute-start | bytes 786440 | tf_op jit(solution)/shard_map/ppermute | solution.py:22
  18.0 25.3 %collective-permute-start.1 = (bf16[2,64,2048]{2,1,0:T(8,128)(2,1)S(1)}, bf16[2,64,2048]{2,1,0:T(8,128)(2,1)S(1)}, u32[]{:S(2)}, u32[]{:S(2)}) collective-permute-start(bf16[2,64,2048]{2,1,0:T(8,128)(2,1)S(1)} %get-tuple-element.7), channel_id=1, source_target_pairs={{0,8},{4,12},{8,0},{12,4},{1,9},{5,13},{9,1},{13,5},{2,10},{6,14},... | collective-permute-start | bytes 1572872 | tf_op jit(solution)/shard_map/ppermute | solution.py:22
  43.7 39.7 %copy-start.1 = (bf16[64,2048]{1,0:T(8,128)(2,1)S(1)}, bf16[64,2048]{1,0:T(8,128)(2,1)}, u32[]{:S(2)}) copy-start(bf16[64,2048]{1,0:T(8,128)(2,1)} %param.6) | copy-start | bytes 786436
  43.7 52.6 %copy-start.2 = (f32[2048]{0:T(1024)S(1)}, f32[2048]{0:T(1024)}, u32[]{:S(2)}) copy-start(f32[2048]{0:T(1024)} %param.8) | copy-start | bytes 24580
  50.8 61.5 %all-gather.3.cloned.1.call-start = ((), (), s32[]{:S(2)}) async-start(), calls=%async_computation.3 | async-start | bytes 1310720 | tf_op jit(solution)/shard_map/all_gather | solution.py:58
  98.2 65.6 %reduce-scatter.5.cloned.1.call-start = ((), (), s32[]{:S(2)}) async-start(), calls=%async_computation.4 | async-start | bytes 2621440 | tf_op jit(solution)/shard_map/reduce_scatter | solution.py:61
  112.3 88.5 %copy-start = (bf16[256,2048]{1,0:T(8,128)(2,1)S(1)}, bf16[256,2048]{1,0:T(8,128)(2,1)}, u32[]{:S(2)}) copy-start(bf16[256,2048]{1,0:T(8,128)(2,1)} %all-gather.3.cloned.1.call-done) | copy-start | bytes 3145732
  119.7 81.0 %all-gather.5.cloned.1.call-start = ((), (), s32[]{:S(2)}) async-start(), calls=%async_computation.5 | async-start | bytes 1310720 | tf_op jit(solution)/shard_map/all_gather | solution.py:69
Sparse Core Ops, SparseCore 0:
  50.9 32.3 reduce-scatter.2
  98.3 13.9 all-gather.2
  119.9 43.8 reduce-scatter.4
  173.9 26.7 all-gather.4
